TPU v7x, 256 devices: a whole 4x4x8 slice. The times are simulated.
256 devices in a mesh: leaf: 64 (over y, z, core), panel: 4 (over x).
Axes of the slice: x: 4, y: 4, z: 8, core: 2. Of those that a mesh axis runs over, the one named last changes fastest.
Arguments:
- sigma_tiles: bfloat16 [1024, 256, 256], P('leaf', 'panel'), may hold values from -6 to 6
- panel_factor: bfloat16 [256, 15, 256, 256], P('leaf', None, 'panel'), may hold values from -0.09375 to 0.09375
- panel_mask: int32 [256, 15], P('leaf'), may hold values 0 or 1
- inv_diagonal: float32 [256, 256], P('leaf', 'panel'), may hold values from 0.5 to 2
- subtree_of: int32 [64], replicated, may hold values from 0 to 15
- partition_order: int32 [65536], P(('leaf', 'panel')), may hold values from 0 to 65535, each once
Outputs:
- covariance: bfloat16 [256, 15, 256, 256], P('leaf', None, 'panel')
- variance: float32 [65536], P(('leaf', 'panel'))
All inputs are finite; a program needn't handle non-finite values. No bound on the sum of `panel_mask` on one device may be relied on, other than what follows from the above.
Results may differ from a plain program's by a relative error of at most 0.00065.
Values may be sent and summed in bfloat16 or wider, within the bound.
A program may use at most 128 MiB of HBM per device.

v0:
```python
import jax
import jax.numpy as jnp
from jax import lax
from jax.sharding import PartitionSpec as P

NA = 32
CH = 15


def chain_blocks(subtree):
    subtree_col = subtree[..., None]
    root_ids = jnp.broadcast_to(jnp.arange(8, dtype=jnp.int32), subtree_col.shape[:-1] + (8,))
    upper_ids = 8 + 4 * (subtree_col // 8) + jnp.arange(4, dtype=jnp.int32)
    middle = 16 + 2 * (subtree_col // 4) + jnp.arange(2, dtype=jnp.int32)
    lower_ids = 24 + subtree_col // 2
    return jnp.concatenate([root_ids, upper_ids, middle, lower_ids], axis=-1)


def path_limit(count):
    return max(count // 32 * 15, min(count, 8) + max(0, min(count, 16) - 8) // 2)


def pick_slots(tile_ids, group_size, my_group, slots):
    in_group = tile_ids // group_size == my_group
    group_rank = jnp.cumsum(in_group.astype(jnp.int32), axis=1) - 1
    wanted = jnp.arange(slots, dtype=jnp.int32)
    chosen = in_group[:, :, None] & (group_rank[:, :, None] == wanted[None, None, :])
    local_ids = jnp.sum(jnp.where(chosen, (tile_ids % group_size)[:, :, None], 0), axis=1)
    filled = jnp.any(chosen, axis=1)
    return (local_ids, filled)


def body(sigma_tiles, panel_factor, panel_mask, inv_diagonal, subtree_of, partition_order):
    leaves = lax.axis_size("leaf")
    panels = lax.axis_size("panel")
    my_leaf = lax.axis_index("leaf")
    owned_count = sigma_tiles.shape[0]
    row_count = sigma_tiles.shape[1]
    width_full = sigma_tiles.shape[2]
    local_desc = panel_factor.shape[0]
    chains = chain_blocks(subtree_of)
    tile_ids = (chains[:, :, None] * NA + chains[:, None, :]).reshape(leaves, CH * CH)
    my_tiles = tile_ids[my_leaf]
    order_idx = jnp.arange(CH * CH)
    earlier = order_idx[None, :] < order_idx[:, None]
    capacity = path_limit(owned_count)
    local_ids, filled = pick_slots(tile_ids, owned_count, my_leaf, capacity)
    outgoing = jnp.take(sigma_tiles, local_ids.reshape(-1), axis=0).reshape(
        leaves, capacity, row_count, width_full
    )
    outgoing = jnp.where(filled[:, :, None, None], outgoing, jnp.zeros_like(outgoing))
    incoming = lax.all_to_all(outgoing, "leaf", split_axis=0, concat_axis=0, tiled=True)
    source = my_tiles // owned_count
    position = jnp.sum(((source[:, None] == source[None, :]) & earlier).astype(jnp.int32), axis=1)
    flat_slot = source * capacity + position
    slot_total = leaves * capacity
    ancestors = jnp.take(incoming.reshape(slot_total, row_count, width_full), flat_slot, axis=0)
    ancestors = ancestors.reshape(CH, CH, row_count, width_full)
    masked = panel_factor * panel_mask[:, :, None, None].astype(jnp.bfloat16)
    product = jnp.einsum(
        "abrk,jbkc->jarc",
        ancestors,
        lax.all_gather(masked, "panel", axis=2, tiled=True),
        preferred_element_type=jnp.float32,
    )
    covariance = (-product).astype(jnp.bfloat16)
    partial_value = jnp.sum(masked.astype(jnp.float32) * product, axis=(1, 2))
    shares = (
        lax.psum_scatter(partial_value, "panel", scatter_dimension=1, tiled=True) + inv_diagonal
    )
    gathered = lax.all_gather(shares, ("leaf", "panel"), axis=0, tiled=True)
    ordered = (
        gathered.reshape(leaves, panels, local_desc, width_full // panels)
        .transpose(0, 2, 1, 3)
        .reshape(-1)
    )
    variance = jnp.take(ordered, partition_order, axis=0)
    return (covariance, variance)


def solution(mesh):
    placed = (
        P("leaf", "panel", None),
        P("leaf", None, "panel", None),
        P("leaf", None),
        P("leaf", "panel"),
        P(),
        P(("leaf", "panel")),
    )
    return jax.shard_map(
        body,
        mesh=mesh,
        in_specs=placed,
        out_specs=(P("leaf", None, "panel", None), P(("leaf", "panel"))),
        check_vma=False,
    )
```

profile of v0, /device:TPU:1, one launch (start us, length us, event | category | flops | bytes accessed | tf_op | source)
XLA Modules:
  0.0 788.5 jit_solution(3469744076644809767)
XLA Ops:
  7.2 0.7 multiply_add_fusion.1
  8.2 0.6 reduce-window.6
  8.8 0.2 slice_reduce_fusion
  9.1 0.3 select_reduce_fusion
  9.5 0.3 fusion.9
  10.0 0.1 copy.51
  10.2 18.1 %gather_fusion = bf16[768,64,256]{2,1,0:T(8,128)(2,1)} fusion(bf16[16,64,256]{2,1,0:T(8,128)(2,1)S(1)} %copy-done, s32[1024]{0:T(1024)S(1)} %pad_clamp_fusion.2), kind=kCustom, calls=%fused_computation | custom fusion | bytes 50334720 | tf_op jit(solution)/shard_map/jit(_take)/gather | solution.py:48
  28.3 21.8 %select_select_fusion = bf16[64,12,64,256]{3,2,1,0:T(8,128)(2,1)} fusion(bf16[64,12,64,256]{3,2,1,0:T(8,128)(2,1)} %bitcast.50, pred[64,12]{1,0:T(8,128)(4,1)S(1)} %copy.51, pred[64,12]{1,0:T(8,128)(4,1)S(1)} %copy.50), kind=kLoop, calls=%fused_computation.3 | loop fusion | flops 25165824 | bytes 50333184 | tf_op jit(solution)/shard_map/jit(_where)/select_n | solution.py:51
  50.1 13.4 %all-to-all-start = ((bf16[64,12,64,256]{3,2,1,0:T(8,128)(2,1)}), bf16[64,12,64,256]{3,2,1,0:T(8,128)(2,1)}, u32[]{:S(2)}, u32[]{:S(2)}) async-start(bf16[64,12,64,256]{3,2,1,0:T(8,128)(2,1)} %select_select_fusion), calls=%async_computation | async-start | bytes 50331648 | tf_op jit(solution)/shard_map/all_to_all | solution.py:52
  63.6 1.5 broadcast_multiply_fusion
  65.1 0.2 reduce-scatter.4.cloned.1.call-start
  65.3 0.2 dynamic-slice_reduce_fusion
  65.7 0.2 convert_reduce_fusion
  66.0 543.1 %all-to-all-done = bf16[64,12,64,256]{3,2,1,0:T(8,128)(2,1)} async-done(((bf16[64,12,64,256]{3,2,1,0:T(8,128)(2,1)}), bf16[64,12,64,256]{3,2,1,0:T(8,128)(2,1)}, u32[]{:S(2)}, u32[]{:S(2)}) %all-to-all-start) | async-done | bytes 25165856 | tf_op jit(solution)/shard_map/all_to_all | solution.py:52
  609.1 16.7 %gather_fusion.1 = bf16[225,64,256]{2,1,0:T(8,128)(2,1)} fusion(bf16[768,64,256]{2,1,0:T(8,128)(2,1)} %bitcast.4, s32[1024]{0:T(1024)S(1)} %pad_clamp_fusion.1), kind=kCustom, calls=%fused_computation.1 | custom fusion | bytes 14746500 | tf_op jit(solution)/shard_map/jit(_take)/gather | solution.py:57
  625.9 13.5 %fusion.6 = (f32[4,256]{1,0:T(4,128)S(1)}, bf16[4,15,64,256]{3,2,1,0:T(8,128)(2,1)}) fusion(bf16[4,15,64,256]{3,2,1,0:T(8,128)(2,1)S(1)} %copy-done.2, bf16[15,15,64,256]{3,2,1,0:T(8,128)(2,1)} %bitcast.51, pred[15,15]{1,0:T(8,128)(4,1)S(1)} %compare_and_fusion.1, bf16[4,15,256,256]{3,2,1,0:T(8,128)(2,1)} %all-gather.3.cloned.1.call-done), kind=kOutput, calls=%fused_computation.12 | convolution fusion | flops 7558347776 | bytes 19173600 | tf_op jit(solution)/shard_map/abrk,jbkc->jarc/dot_general | solution.py:60
  639.4 0.8 copy.56
  640.2 19.6 %reduce-scatter.4.cloned.1.call-done = f32[64,4]{1,0:T(8,128)} async-done(((f32[256,4]{1,0:T(8,128)}), f32[64,4]{1,0:T(8,128)}) %reduce-scatter.4.cloned.1.call-update) | async-done | bytes 1040
  659.8 0.8 copy.57
  660.6 118.3 %all-gather = f32[256,4,64]{2,1,0:T(4,128)S(1)} all-gather(f32[1,4,64]{2,1,0:T(4,128)S(1)} %add_bitcast_fusion.1), channel_id=1, replica_groups=mesh['leaf'=64,'panel'=4] {'leaf','panel'}, dimensions={0}, use_global_device_ids=true | all-gather | bytes 263168 | tf_op jit(solution)/shard_map/all_gather | solution.py:71
  778.9 0.1 copy.63
  779.1 0.3 reshape.336
  779.3 1.7 gather_fusion.2
  781.1 0.6 and_select_fusion.1
  (47 shorter events, 1.0 us)
Async XLA Ops:
  7.2 3.1 copy-start
  50.1 13.5 %copy-start.6 = (s32[4,15]{1,0:T(4,128)S(1)}, s32[4,15]{1,0:T(4,128)}, u32[]{:S(2)}) copy-start(s32[4,15]{1,0:T(4,128)} %param.8) | copy-start | bytes 724
  50.1 13.5 %copy-start.3 = (bf16[4,15,64,256]{3,2,1,0:T(8,128)(2,1)S(1)}, bf16[4,15,64,256]{3,2,1,0:T(8,128)(2,1)}, u32[]{:S(2)}) copy-start(bf16[4,15,64,256]{3,2,1,0:T(8,128)(2,1)} %param.7) | copy-start | bytes 5898244
  50.1 15.9 %copy-start.4 = (s32[256]{0:T(256)S(1)}, s32[256]{0:T(256)}, u32[]{:S(2)}) copy-start(s32[256]{0:T(256)} %param.11) | copy-start | bytes 3076
  50.1 559.1 %all-to-all-start = ((bf16[64,12,64,256]{3,2,1,0:T(8,128)(2,1)}), bf16[64,12,64,256]{3,2,1,0:T(8,128)(2,1)}, u32[]{:S(2)}, u32[]{:S(2)}) async-start(bf16[64,12,64,256]{3,2,1,0:T(8,128)(2,1)} %select_select_fusion), calls=%async_computation | async-start | bytes 50331648 | tf_op jit(solution)/shard_map/all_to_all | solution.py:52
  63.5 562.3 %all-gather.3.cloned.1.call-start = ((), (), s32[]{:S(2)}) async-start(), calls=%async_computation.2 | async-start | bytes 9830400 | tf_op jit(solution)/shard_map/all_gather | solution.py:63
  65.1 594.7 %reduce-scatter.4.cloned.1.call-start = ((), (), s32[]{:S(2)}) async-start(), calls=%async_computation.3 | async-start | bytes 163840
  609.1 16.7 %copy-start.2 = (bf16[4,15,64,256]{3,2,1,0:T(8,128)(2,1)S(1)}, bf16[4,15,64,256]{3,2,1,0:T(8,128)(2,1)}, u32[]{:S(2)}) copy-start(bf16[4,15,64,256]{3,2,1,0:T(8,128)(2,1)} %broadcast_multiply_fusion) | copy-start | bytes 5898244
  625.9 34.7 %copy-start.5 = (f32[4,64]{1,0:T(4,128)S(1)}, f32[4,64]{1,0:T(4,128)}, u32[]{:S(2)}) copy-start(f32[4,64]{1,0:T(4,128)} %param.9) | copy-start | bytes 3076
  625.9 155.8 %copy-start.1 = (bf16[16,64,256]{2,1,0:T(8,128)(2,1)S(1)}, bf16[16,64,256]{2,1,0:T(8,128)(2,1)}, u32[]{:S(2)}) copy-start(bf16[16,64,256]{2,1,0:T(8,128)(2,1)} %param.6) | copy-start | bytes 1572868
Sparse Core Ops, SparseCore 0:
  66.7 82.2 all-gather.2
  640.3 19.4 reduce-scatter.3
where the time goes:
time: 790 us; the launch traced here: 788 us
  waiting for transfers between devices  563 us (71%)
  blocking collectives  118 us (15%)
  local copies, waits for them, and re-layouts  39.4 us (5%)
  other arithmetic  26.5 us (3%)
  between operations  14.3 us (2%)
  starting transfers between devices  13.7 us (2%)
  matrix products  13.5 us (2%)
    all_to_all x1, waiting for transfers between devices, body(): lax.all_to_all(outgoing, 'leaf', split_axis=0, concat_axis=0, tiled=True)  543 us
    all_gather x1, blocking collectives, body(): gathered = lax.all_gather(shares, ('leaf', 'panel'), axis=0, tiled=True)  118 us
    select_n x1, other arithmetic, body(): jnp.where(filled[:, :, None, None], outgoing, jnp.zeros_like(outgoing))  21.8 us
    unnamed x3, waiting for transfers between devices  19.6 us
    gather x1, local copies, waits for them, and re-layouts, body(): jnp.take(sigma_tiles, local_ids.reshape(-1), axis=0)  18.1 us
    gather x1, local copies, waits for them, and re-layouts, body(): jnp.take(incoming.reshape(slot_total, row_count, width_full), flat_slot,...  16.7 us
  transfers between devices with their start and end apart: 3, of which 2 were waited for; matrix products, arithmetic and copies ran while one was open for 2% of the time, Pallas kernels for 0%

commit v1 on v0

v1 whole, which is shorter than its diff:
```python
import jax
import jax.numpy as jnp
from jax import lax
from jax.experimental import pallas as pl
from jax.experimental.pallas import tpu as pltpu
from jax.sharding import PartitionSpec as P

NX, NY, NZ = 4, 4, 8
CH = 15
B = 256
Q = 64
DESC = 4
NEAR = 12
FAR = (20, 8, 4, 3)
FAR_AT = (0, 20, 28, 32)
COLUMN = 35
FAR_BASE = NX * NY * NZ // NX * NEAR
TILES = FAR_BASE + NZ * COLUMN
Z_ORDER = (0, -1, 1, -2, 2, -3, 3, 4)
GROUP = 5
MESH = pl.DeviceIdType.MESH


def halves(count):
    return (0, (count + 1) // 2), ((count + 1) // 2, count // 2)


def kernel(
    idx_ref, mask_ref, inv_ref, sigma_ref, factor_ref,
    cov_ref, table_ref,
    tiles, lhs, full, own, parts, table,
    send_sem, recv_sem, local_sem,
):
    leaf = lax.axis_index("leaf")
    x = lax.axis_index("panel")
    core = lax.rem(leaf, 2)
    chip = leaf // 2
    y = chip // NZ
    z = lax.rem(chip, NZ)

    def mod(value, size):
        return lax.rem(value + 2 * size, size)

    def at(dy=0, dz=0, dc=0):
        return {"leaf": (mod(y + dy, NY) * NZ + mod(z + dz, NZ)) * 2 + lax.rem(core + dc, 2), "panel": x}

    def beside(dx):
        return {"leaf": leaf, "panel": mod(x + dx, NX)}

    sends = {}
    recvs = {}
    pending = []

    def number(names, name):
        if name not in names:
            names[name] = len(names)
        return names[name]

    def copy(src, dst, device, name):
        return pltpu.make_async_remote_copy(
            src_ref=src, dst_ref=dst,
            send_sem=send_sem.at[number(sends, name)],
            recv_sem=recv_sem.at[number(recvs, name)],
            device_id=device, device_id_type=MESH,
        )

    def send(ref, device, name, src=None):
        def build():
            return copy((src or ref)(), ref(), device(), name)

        build().start()
        pending.append(build)

    def arrive(ref, name):
        copy(ref, ref, beside(1), name).wait_recv()

    for j in range(DESC):
        pltpu.make_async_copy(factor_ref.at[j], own.at[j], local_sem.at[j]).start()

    peers = (
        [beside(d) for d in range(1, NX)]
        + [at(dz=d) for d in range(1, NZ)]
        + [at(dy=d, dc=c) for d in range(NY) for c in range(2) if (d, c) != (0, 0)]
    )
    barrier = pltpu.get_barrier_semaphore()
    for peer in peers:
        pl.semaphore_signal(barrier, inc=1, device_id=peer, device_id_type=MESH)
    pl.semaphore_wait(barrier, len(peers))

    def quarter(j, dx, low=0, count=CH):
        return full.at[j, pl.ds(low, count), pl.ds(pl.multiple_of(mod(x + dx, NX) * Q, Q), Q)]

    def factor_parts(j):
        first = 8 - j % 2
        return (0, first), (first, CH - first)

    def factor_start(j):
        pltpu.make_async_copy(factor_ref.at[j], own.at[j], local_sem.at[j]).wait()
        for b in range(CH):
            own[j, b] = own[j, b] * mask_ref[j, b].astype(jnp.bfloat16)
        send(lambda: quarter(j, 0), lambda: beside(1), ("fr", j), src=lambda: own.at[j])
        send(lambda: quarter(j, 0), lambda: beside(-1), ("fl", j), src=lambda: own.at[j])
        pltpu.make_async_copy(own.at[j], quarter(j, 0), local_sem.at[DESC + j]).start()

    def factor_forward(j):
        right, left = factor_parts(j)
        arrive(quarter(j, -1), ("fr", j))
        send(lambda: quarter(j, -1, *right), lambda: beside(1), ("fr2", j))
        arrive(quarter(j, 1), ("fl", j))
        send(lambda: quarter(j, 1, *left), lambda: beside(-1), ("fl2", j))

    def factor_done(j):
        right, left = factor_parts(j)
        arrive(quarter(j, 2, *right), ("fr2", j))
        arrive(quarter(j, 2, *left), ("fl2", j))
        pltpu.make_async_copy(own.at[j], quarter(j, 0), local_sem.at[DESC + j]).wait()

    def near(dy, dz, low=0, count=NEAR):
        row = mod(y + dy, NY) * NZ + mod(z + dz, NZ)
        return tiles.at[pl.ds(row * NEAR + low, count)]

    def far(dz, low=0, count=COLUMN):
        return tiles.at[pl.ds(FAR_BASE + mod(z + dz, NZ) * COLUMN + low, count)]

    first6, last6 = halves(NEAR)
    near_chunks = [(dy, dz) for dy in range(NY) for dz in Z_ORDER]

    def run_core0():
        def to_peer(dy, dz):
            send(lambda: near(dy, dz), lambda: at(dc=1), ("n", dy % NY, dz))

        def along_y(dz):
            send(lambda: near(0, dz), lambda: at(dy=1), ("yu", dz))
            send(lambda: near(0, dz), lambda: at(dy=-1), ("yd", dz))
            to_peer(0, dz)

        def start():
            @pl.when(y == 0)
            def _():
                ref = far(0, 0, 4)
                copy(sigma_ref.at[pl.ds(12, 4)], ref, at(dc=1), ("extra",)).start()

            upper = jnp.where(y == 0, 0, z // 4)
            one = pltpu.make_async_copy(sigma_ref.at[pl.ds(0, 8)], near(0, 0, 0, 8), local_sem.at[2 * DESC])
            two = pltpu.make_async_copy(
                sigma_ref.at[pl.ds(8 + 4 * upper, 4)], near(0, 0, 8, 4), local_sem.at[2 * DESC + 1]
            )
            one.start()
            two.start()
            one.wait()
            two.wait()
            send(lambda: near(0, 0), lambda: at(dz=1), ("zr", 1))
            send(lambda: near(0, 0), lambda: at(dz=-1), ("zl", 1))
            along_y(0)

        def ring(d):
            arrive(near(0, -d), ("zr", d))
            if d < 3:
                send(lambda: near(0, -d), lambda: at(dz=1), ("zr", d + 1))
            else:
                send(lambda: near(0, -d, *first6), lambda: at(dz=1), ("zr", 4))
            arrive(near(0, d), ("zl", d))
            if d < 3:
                send(lambda: near(0, d), lambda: at(dz=-1), ("zl", d + 1))
            else:
                send(lambda: near(0, d, *last6), lambda: at(dz=-1), ("zl", 4))
            along_y(-d)
            along_y(d)

        def ring_end():
            arrive(near(0, 4, *first6), ("zr", 4))
            arrive(near(0, 4, *last6), ("zl", 4))
            along_y(4)

        def cross(dz):
            arrive(near(-1, dz), ("yu", dz))
            send(lambda: near(-1, dz, *first6), lambda: at(dy=1), ("yu2", dz))
            arrive(near(1, dz), ("yd", dz))
            send(lambda: near(1, dz, *last6), lambda: at(dy=-1), ("yd2", dz))
            to_peer(-1, dz)
            to_peer(1, dz)

        def cross_end(dz):
            arrive(near(2, dz, *first6), ("yu2", dz))
            arrive(near(2, dz, *last6), ("yd2", dz))
            to_peer(2, dz)

        events = [(0, 0, start), (0, 1, lambda: factor_start(0))]
        events += [(0, 2 + j, lambda j=j: factor_start(j)) for j in range(1, DESC)]
        events += [(5 * d, 1, lambda d=d: ring(d)) for d in range(1, 4)]
        events += [(17, 1, ring_end)]
        for k, dz in enumerate(Z_ORDER):
            events += [(6 * (k + 1), 2, lambda dz=dz: cross(dz)), (6 * (k + 2), 3, lambda dz=dz: cross_end(dz))]
        events += [(15 * j + 11, 4, lambda j=j: factor_forward(j)) for j in range(DESC)]
        for _, _, event in sorted(events, key=lambda e: e[:2]):
            event()
        for dz in Z_ORDER:
            arrive(far(dz, 0, FAR[0]), ("a", dz))
            arrive(far(dz, FAR[0], COLUMN - FAR[0]), ("b", dz))
        for op in pending:
            op().wait_send()

        @pl.when(y == 0)
        def _():
            copy(sigma_ref.at[pl.ds(12, 4)], far(0, 0, 4), at(dc=1), ("extra",)).wait_send()

    def run_core1():
        piece = {"a": (0, FAR[0]), "b": (FAR[0], COLUMN - FAR[0])}

        def sub(name, which):
            low, count = piece[name]
            at_low, at_count = halves(count)[which]
            return (low + at_low, at_count)

        def around(name):
            send(lambda: far(0, *piece[name]), lambda: at(dz=1), ("zr" + name, 1))
            send(lambda: far(0, *piece[name]), lambda: at(dz=-1), ("zl" + name, 1))
            send(lambda: far(0, *piece[name]), lambda: at(dc=1), (name, 0))

        later = []

        def only(condition, action):
            before = len(pending)

            @pl.when(condition)
            def _():
                action()

            for op in pending[before:]:
                later.append((condition, op))
            del pending[before:]

        def load_own(c):
            if c == 0:
                pieces = [(0, 4, 16)]
            elif c == 1:
                pieces = [(4 * (z // 4), 20, 4), (8 + 4 * (z // 4), 24, 4)]
            elif c == 2:
                pieces = [(2 * (z // 2), 28, 2), (8 + 2 * (z // 2), 30, 2)]
            else:
                pieces = [(2 * (z // 2), 32, 2), (8 + z, 34, 1)]
            ops = [
                pltpu.make_async_copy(
                    sigma_ref.at[pl.ds(src, count)], far(0, dst, count), local_sem.at[2 * DESC + k]
                )
                for k, (src, dst, count) in enumerate(pieces)
            ]
            for op in ops:
                op.start()
            for op in ops:
                op.wait()
            if c == 0:
                arrive(far(0, 0, 4), ("extra",))
            send(lambda: far(0, FAR_AT[c], FAR[c]), lambda: at(dy=1), ("cu",))
            send(lambda: far(0, FAR_AT[c], FAR[c]), lambda: at(dy=-1), ("cd",))

        def from_below(c):
            low, count = halves(FAR[c])[0]
            arrive(far(0, FAR_AT[c], FAR[c]), ("cu",))
            send(lambda: far(0, FAR_AT[c] + low, count), lambda: at(dy=1), ("cu2",))

        def from_above(c):
            low, count = halves(FAR[c])[1]
            arrive(far(0, FAR_AT[c], FAR[c]), ("cd",))
            send(lambda: far(0, FAR_AT[c] + low, count), lambda: at(dy=-1), ("cd2",))

        def from_two(c):
            for (low, count), name in zip(halves(FAR[c]), (("cu2",), ("cd2",))):
                arrive(far(0, FAR_AT[c] + low, count), name)

        def start():
            for c in range(NY):
                only(y == c, lambda c=c: load_own(c))

        def across():
            for c in range(NY):
                only(y == (c + 1) % NY, lambda c=c: from_below(c))
            for c in range(NY):
                only(y == (c - 1) % NY, lambda c=c: from_above(c))
            only(y != 2, lambda: around("a"))

        def across_end():
            for c in range(NY):
                only(y == (c + 2) % NY, lambda c=c: from_two(c))
            only(y == 2, lambda: around("a"))
            around("b")

        def ring(name, d):
            arrive(far(-d, *piece[name]), ("zr" + name, d))
            right = piece[name] if d < 3 else sub(name, 0)
            send(lambda: far(-d, *right), lambda: at(dz=1), ("zr" + name, d + 1))
            arrive(far(d, *piece[name]), ("zl" + name, d))
            left = piece[name] if d < 3 else sub(name, 1)
            send(lambda: far(d, *left), lambda: at(dz=-1), ("zl" + name, d + 1))
            send(lambda: far(-d, *piece[name]), lambda: at(dc=1), (name, -d))
            send(lambda: far(d, *piece[name]), lambda: at(dc=1), (name, d))

        def ring_end(name):
            arrive(far(4, *sub(name, 0)), ("zr" + name, 4))
            arrive(far(4, *sub(name, 1)), ("zl" + name, 4))
            send(lambda: far(4, *piece[name]), lambda: at(dc=1), (name, 4))

        events = [(0, 0, start), (0, 1, lambda: factor_start(0))]
        events += [(0, 2 + j, lambda j=j: factor_start(j)) for j in range(1, DESC)]
        events += [(5, 1, across), (8, 1, across_end)]
        for k, name in enumerate("ab"):
            events += [(11 + 12 * d + 5 * k, 1, lambda d=d, name=name: ring(name, d)) for d in range(1, 4)]
            events += [(54 + k, 1, lambda name=name: ring_end(name))]
        events += [(15 * j + 11, 4, lambda j=j: factor_forward(j)) for j in range(DESC)]
        for _, _, event in sorted(events, key=lambda e: e[:2]):
            event()
        for dy, dz in near_chunks:
            arrive(near(dy, dz), ("n", dy, dz))
        for op in pending:
            op().wait_send()
        for condition, op in later:
            @pl.when(condition)
            def _():
                op().wait_send()

    @pl.when(core == 0)
    def _():
        run_core0()

    pending.clear()

    @pl.when(core == 1)
    def _():
        run_core1()

    pending.clear()

    @pl.loop(0, CH)
    def _(a):
        for b in range(CH):
            lhs[pl.ds(pl.multiple_of(a * Q, Q), Q), pl.ds(b * B, B)] = tiles[idx_ref[a * CH + b]]

    for j in range(DESC):
        factor_done(j)

    for j in range(DESC):
        rhs = full[j].reshape(CH * B, B)

        def step(g, total):
            rows = pl.ds(pl.multiple_of(g * GROUP * Q, Q), GROUP * Q)
            product = jnp.dot(lhs[rows, :], rhs, preferred_element_type=jnp.float32)
            product = product.reshape(GROUP, Q, B)
            blocks = pl.ds(g * GROUP, GROUP)
            cov_ref[j, blocks] = (-product).astype(jnp.bfloat16)
            return total + jnp.sum(own[j, blocks].astype(jnp.float32) * product, axis=(0, 1), keepdims=True)[0]

        total = lax.fori_loop(0, CH // GROUP, step, jnp.zeros((1, B), jnp.float32))
        parts[x, pl.ds(j, 1)] = total + inv_ref[pl.ds(j, 1)]

    for d in range(1, NX):
        send(lambda: parts.at[x], lambda d=d: beside(d), ("vx", d))
    for d in range(1, NX):
        arrive(parts.at[mod(x - d, NX)], ("vx", d))
    mine = table.at[z, y, core]
    mine[...] = (parts[0] + parts[1]) + (parts[2] + parts[3])
    pairs = [(dy, dc) for dy in range(NY) for dc in range(2) if (dy, dc) != (0, 0)]
    for dy, dc in pairs:
        send(lambda: mine, lambda dy=dy, dc=dc: at(dy=dy, dc=dc), ("vy", dy, dc))
    for dy, dc in pairs:
        arrive(table.at[z, mod(y - dy, NY), lax.rem(core + dc, 2)], ("vy", dy, dc))
    for dz in range(1, NZ):
        send(lambda: table.at[z], lambda dz=dz: at(dz=dz), ("vz", dz))
    for dz in range(1, NZ):
        arrive(table.at[mod(z - dz, NZ)], ("vz", dz))
    table_ref[...] = table[...]
    for op in pending:
        op().wait_send()
    assert len(sends) <= SEMS and len(recvs) <= SEMS


SEMS = 240


def tile_slots(subtree):
    upper, middle, lower = subtree // 8, subtree // 4, subtree // 2
    i4 = jnp.arange(4, dtype=jnp.int32)
    i2 = jnp.arange(2, dtype=jnp.int32)
    i8 = jnp.arange(8, dtype=jnp.int32)
    rows = jnp.concatenate([i8, 8 + 4 * upper + i4, 16 + 2 * middle + i2, 24 + lower[None]])
    z = rows % 8
    base = FAR_BASE + z * COLUMN
    near_part = rows[:, None] * NEAR + jnp.arange(NEAR, dtype=jnp.int32)
    first = jnp.where(upper == 0, near_part[:8], jnp.concatenate(
        [near_part[:8, :8], base[:8, None] + i4], axis=1))
    near_part = jnp.concatenate([first, near_part[8:]], axis=0)
    far0 = base[:8, None] + jnp.concatenate([4 + 2 * middle + i2, 12 + lower[None]])
    far1 = base[8:12, None] + jnp.concatenate(
        [20 + 2 * (middle - 2 * upper) + i2, 24 + (lower - 4 * upper)[None]])
    far2 = base[12:14, None] + jnp.concatenate([28 + i2, 30 + (lower - 2 * middle)[None]])
    far3 = base[14:, None] + jnp.arange(32, 35, dtype=jnp.int32)
    far_part = jnp.concatenate([far0, far1, far2, far3], axis=0)
    return jnp.concatenate([near_part, far_part], axis=1).reshape(-1).astype(jnp.int32)


def body(sigma_tiles, panel_factor, panel_mask, inv_diagonal, subtree_of, partition_order):
    leaf = lax.axis_index("leaf")
    x = lax.axis_index("panel")
    slots = tile_slots(subtree_of[leaf])
    mine = (jnp.arange(B) // Q == x)[None, :]
    inverse = jnp.where(mine, jnp.tile(inv_diagonal, (1, NX)), 0.0)
    covariance, table = pl.pallas_call(
        kernel,
        out_shape=(
            jax.ShapeDtypeStruct((DESC, CH, Q, B), jnp.bfloat16),
            jax.ShapeDtypeStruct((NZ, NY, 2, DESC, B), jnp.float32),
        ),
        in_specs=[
            pl.BlockSpec(memory_space=pltpu.SMEM),
            pl.BlockSpec(memory_space=pltpu.SMEM),
            pl.BlockSpec(memory_space=pltpu.VMEM),
            pl.BlockSpec(memory_space=pl.ANY),
            pl.BlockSpec(memory_space=pl.ANY),
        ],
        out_specs=(
            pl.BlockSpec(memory_space=pltpu.VMEM),
            pl.BlockSpec(memory_space=pltpu.VMEM),
        ),
        scratch_shapes=[
            pltpu.VMEM((TILES, Q, B), jnp.bfloat16),
            pltpu.VMEM((CH * Q, CH * B), jnp.bfloat16),
            pltpu.VMEM((DESC, CH, B, B), jnp.bfloat16),
            pltpu.VMEM((DESC, CH, Q, B), jnp.bfloat16),
            pltpu.VMEM((NX, DESC, B), jnp.float32),
            pltpu.VMEM((NZ, NY, 2, DESC, B), jnp.float32),
            pltpu.SemaphoreType.DMA((SEMS,)),
            pltpu.SemaphoreType.DMA((SEMS,)),
            pltpu.SemaphoreType.DMA((2 * DESC + 2,)),
        ],
        compiler_params=pltpu.CompilerParams(
            collective_id=0, has_side_effects=True, vmem_limit_bytes=58 * 1024 * 1024
        ),
    )(slots, panel_mask, inverse, sigma_tiles, panel_factor)
    column = partition_order % B
    block = partition_order // B
    owner, j = block // DESC, block % DESC
    place = (((owner // 2 % NZ * NY + owner // 2 // NZ) * 2 + owner % 2) * DESC + j) * B + column
    variance = jnp.take(table.reshape(-1), place, axis=0)
    return covariance, variance


def solution(mesh):
    placed = (
        P("leaf", "panel", None),
        P("leaf", None, "panel", None),
        P("leaf", None),
        P("leaf", "panel"),
        P(),
        P(("leaf", "panel")),
    )
    return jax.shard_map(
        body,
        mesh=mesh,
        in_specs=placed,
        out_specs=(P("leaf", None, "panel", None), P(("leaf", "panel"))),
        check_vma=False,
    )
```

time: 790 us -> 131 us (0.17)
  waiting for transfers between devices: 563 us -> 0 us
  blocking collectives: 118 us -> 0 us
  Pallas kernels: 0 us -> 115 us
  local copies, waits for them, and re-layouts: 39.4 us -> 9.36 us
  other arithmetic: 26.5 us -> 2.86 us
  starting transfers between devices: 13.7 us -> 0 us
  matrix products: 13.5 us -> 0 us
  between operations: 14.3 us -> 3.37 us
    all_to_all x1 -> x0, waiting for transfers between devices: 543 us -> none  [body(): lax.all_to_all(outgoing, 'leaf', split_axis=0, concat_axis=0, tiled=True)]
    all_gather x1 -> x0, blocking collectives: 118 us -> none  [body(): gathered = lax.all_gather(shares, ('leaf', 'panel'), axis=0, tiled=True)]
    pallas_call x0 -> x1, Pallas kernels: none -> 115 us  [body(): pl.pallas_call(kernel, out_shape=(jax.ShapeDtypeStruct((DESC, CH, Q, B),...]
    gather x3 -> x1, local copies, waits for them, and re-layouts: 36.5 us -> 1.72 us  [body(): variance = jnp.take(table.reshape(-1), place, axis=0)]
    select_n x7 -> x4, other arithmetic: 22.4 us -> 1.33 us  [the longest x2 0.65 us: body(): variance = jnp.take(table.reshape(-1), place, axis=0)]
    unnamed x3 -> x0, waiting for transfers between devices: 19.6 us -> none
    dot_general x1 -> x0, matrix products: 13.5 us -> none  [body(): jnp.einsum('abrk,jbkc->jarc', ancestors, lax.all_gather(masked, 'panel',...]
    all_to_all x1 -> x0, starting transfers between devices: 13.4 us -> none  [body(): lax.all_to_all(outgoing, 'leaf', split_axis=0, concat_axis=0, tiled=True)]
  transfers between devices with their start and end apart: 3 -> 0, of which waited for: 2 -> 0; matrix products, arithmetic and copies ran while one was open for 2% -> 0% of each run, Pallas kernels for 0% -> 0%
where the time goes in v1:
time: 131 us
  Pallas kernels  115 us (88%)
  local copies, waits for them, and re-layouts  9.36 us (7%)
  between operations  3.37 us (3%)
  other arithmetic  2.86 us (2%)
    pallas_call x1, Pallas kernels, body(): pl.pallas_call(kernel, out_shape=(jax.ShapeDtypeStruct((DESC, CH, Q, B),...  115 us
    unnamed x4, local copies, waits for them, and re-layouts  4.13 us

profile of v1, /device:TPU:1, one launch (start us, length us, event | category | flops | bytes accessed | tf_op | source)
XLA Modules:
  0.0 131.0 jit_solution(3134789700150268128)
XLA Ops:
  0.6 1.2 dynamic_slice.3
  4.6 0.1 broadcast_multiply_fusion
  4.7 0.1 iota_add_fusion
  4.8 0.1 slice_select_fusion
  4.9 0.1 pad_add_fusion.3
  5.0 0.1 broadcast_add_fusion.2
  5.1 0.1 pad_add_fusion.4
  5.2 0.1 broadcast_add_fusion.1
  5.3 0.1 pad_add_fusion.5
  5.4 0.1 broadcast_add_fusion
  5.5 0.6 slice.28
  6.1 0.6 add_add_fusion
  6.8 0.1 pad_add_fusion.1
  6.8 0.1 copy.8
  6.9 0.1 pad_add_fusion
  7.0 0.7 reshape.86.idx_ref
  7.7 0.7 tile.4
  8.4 0.1 tile.10
  8.4 0.6 broadcast_select_fusion.inv_ref
  9.0 115.4 %shard_map.77 = (bf16[4,15,64,256]{3,2,1,0:T(8,128)(2,1)}, f32[8,4,2,4,256]{4,3,2,1,0:T(4,128)}) custom-call(s32[225]{0:T(256)} %reshape.86.idx_ref, s32[4,15]{1,0:T(4,128)} %mask_ref.1, f32[4,256]{1,0:T(4,128)} %broadcast_select_fusion.inv_ref, bf16[16,64,256]{2,1,0:T(8,128)(2,1)} %sigma_ref.1, bf16[4,15,64,256]{3,2,1,0:T(8,128)(2,1)} %factor_ref.1), custom_call_target="tpu_custom_call" | custom-call | tf_op jit(solution)/shard_map/pallas_call | solution.py:406
  124.4 1.1 copy.9
  125.6 1.7 %gather_fusion = f32[256]{0:T(256)S(1)} fusion(f32[65536]{0:T(1024)S(1)} %bitcast.9, s32[1024]{0:T(1024)S(1)} %pad_clamp_fusion), kind=kCustom, calls=%fused_computation | custom fusion | bytes 3072 | tf_op jit(solution)/shard_map/jit(_take)/gather | solution.py:442
  127.3 0.6 and_select_fusion
  127.9 3.0 %copy.11 = bf16[4,15,64,256]{3,2,1,0:T(8,128)(2,1)} copy(bf16[4,15,64,256]{3,2,1,0:T(8,128)(2,1)} %get-tuple-element.10) | data formatting | bytes 3932160
  (17 shorter events, 0.3 us)
Async XLA Ops:
  0.6 124.9 %copy-start = (s32[256]{0:T(256)S(1)}, s32[256]{0:T(256)}, u32[]{:S(2)}) copy-start(s32[256]{0:T(256)} %param.11) | copy-start | bytes 3076

commit v2 on v1

--- a/solution.py
+++ b/solution.py
@@ -17,7 +17,6 @@
 FAR_BASE = NX * NY * NZ // NX * NEAR
 TILES = FAR_BASE + NZ * COLUMN
 Z_ORDER = (0, -1, 1, -2, 2, -3, 3, 4)
-GROUP = 5
 MESH = pl.DeviceIdType.MESH
 
 
@@ -26,8 +25,8 @@
 
 
 def kernel(
-    idx_ref, mask_ref, inv_ref, sigma_ref, factor_ref,
-    cov_ref, table_ref,
+    subtree_ref, mask_ref, inv_ref, order_ref, sigma_ref, factor_ref,
+    product_ref, variance_ref,
     tiles, lhs, full, own, parts, table,
     send_sem, recv_sem, local_sem,
 ):
@@ -77,11 +76,7 @@
     for j in range(DESC):
         pltpu.make_async_copy(factor_ref.at[j], own.at[j], local_sem.at[j]).start()
 
-    peers = (
-        [beside(d) for d in range(1, NX)]
-        + [at(dz=d) for d in range(1, NZ)]
-        + [at(dy=d, dc=c) for d in range(NY) for c in range(2) if (d, c) != (0, 0)]
-    )
+    peers = [beside(1), beside(-1), at(dy=1), at(dy=-1), at(dz=1), at(dz=-1), at(dc=1)]
     barrier = pltpu.get_barrier_semaphore()
     for peer in peers:
         pl.semaphore_signal(barrier, inc=1, device_id=peer, device_id_type=MESH)
@@ -96,8 +91,11 @@
 
     def factor_start(j):
         pltpu.make_async_copy(factor_ref.at[j], own.at[j], local_sem.at[j]).wait()
-        for b in range(CH):
+
+        @pl.loop(0, CH)
+        def _(b):
             own[j, b] = own[j, b] * mask_ref[j, b].astype(jnp.bfloat16)
+
         send(lambda: quarter(j, 0), lambda: beside(1), ("fr", j), src=lambda: own.at[j])
         send(lambda: quarter(j, 0), lambda: beside(-1), ("fl", j), src=lambda: own.at[j])
         pltpu.make_async_copy(own.at[j], quarter(j, 0), local_sem.at[DESC + j]).start()
@@ -330,88 +328,107 @@
 
     pending.clear()
 
-    @pl.loop(0, CH)
+    subtree = subtree_ref[leaf]
+    upper, middle, lower = subtree // 8, subtree // 4, subtree // 2
+
+    def place(a, row, slots):
+        for b, slot in enumerate(slots):
+            lhs[pl.ds(pl.multiple_of(a * Q, Q), Q), pl.ds(b * B, B)] = tiles[slot]
+
+    def near_slots(row, count):
+        return [row * NEAR + k for k in range(count)]
+
+    def column(row):
+        return FAR_BASE + lax.rem(row, NZ) * COLUMN
+
+    @pl.loop(0, 8)
     def _(a):
-        for b in range(CH):
-            lhs[pl.ds(pl.multiple_of(a * Q, Q), Q), pl.ds(b * B, B)] = tiles[idx_ref[a * CH + b]]
-
-    for j in range(DESC):
-        factor_done(j)
-
-    for j in range(DESC):
-        rhs = full[j].reshape(CH * B, B)
-
-        def step(g, total):
-            rows = pl.ds(pl.multiple_of(g * GROUP * Q, Q), GROUP * Q)
-            product = jnp.dot(lhs[rows, :], rhs, preferred_element_type=jnp.float32)
-            product = product.reshape(GROUP, Q, B)
-            blocks = pl.ds(g * GROUP, GROUP)
-            cov_ref[j, blocks] = (-product).astype(jnp.bfloat16)
-            return total + jnp.sum(own[j, blocks].astype(jnp.float32) * product, axis=(0, 1), keepdims=True)[0]
-
-        total = lax.fori_loop(0, CH // GROUP, step, jnp.zeros((1, B), jnp.float32))
-        parts[x, pl.ds(j, 1)] = total + inv_ref[pl.ds(j, 1)]
+        base = column(a)
+        mine = jnp.where(upper == 0, a * NEAR + 8, base)
+        slots = near_slots(a, 8) + [mine + k for k in range(4)]
+        place(a, a, slots + [base + 4 + 2 * middle, base + 5 + 2 * middle, base + 12 + lower])
+
+    @pl.loop(0, 4)
+    def _(i):
+        row = 8 + 4 * upper + i
+        base = column(row) + FAR_AT[1]
+        pair = base + 2 * (middle - 2 * upper)
+        place(8 + i, row, near_slots(row, NEAR) + [pair, pair + 1, base + 4 + lower - 4 * upper])
+
+    @pl.loop(0, 2)
+    def _(i):
+        row = 16 + 2 * middle + i
+        base = column(row) + FAR_AT[2]
+        place(12 + i, row, near_slots(row, NEAR) + [base, base + 1, base + 2 + lower - 2 * middle])
+
+    row = 24 + lower
+    base = column(row) + FAR_AT[3]
+    place(14, row, near_slots(row, NEAR) + [base, base + 1, base + 2])
+
+    spot = lax.broadcasted_iota(jnp.int32, (1, HALF), 1) // Q
+
+    @pl.loop(0, DESC)
+    def _(j):
+        for k in range(DESC):
+            @pl.when(j == k)
+            def _():
+                factor_done(k)
+
+        product = jnp.dot(lhs[...], full[j].reshape(CH * B, B), preferred_element_type=jnp.float32)
+        product = product.reshape(CH, Q, B)
+        product_ref[j] = product.astype(jnp.bfloat16)
+        total = jnp.sum(own[j].astype(jnp.float32) * product, axis=(0, 1), keepdims=True)[0]
+        inverse = inv_ref[pl.ds(j, 1)]
+        inverse = jnp.concatenate([inverse, inverse], axis=1)
+        for half in range(2):
+            share = jnp.where(spot + 2 * half == x, inverse, 0.0)
+            parts[x, pl.ds(2 * j + half, 1)] = total[:, half * HALF:(half + 1) * HALF] + share
 
     for d in range(1, NX):
         send(lambda: parts.at[x], lambda d=d: beside(d), ("vx", d))
     for d in range(1, NX):
         arrive(parts.at[mod(x - d, NX)], ("vx", d))
-    mine = table.at[z, y, core]
-    mine[...] = (parts[0] + parts[1]) + (parts[2] + parts[3])
-    pairs = [(dy, dc) for dy in range(NY) for dc in range(2) if (dy, dc) != (0, 0)]
-    for dy, dc in pairs:
-        send(lambda: mine, lambda dy=dy, dc=dc: at(dy=dy, dc=dc), ("vy", dy, dc))
-    for dy, dc in pairs:
-        arrive(table.at[z, mod(y - dy, NY), lax.rem(core + dc, 2)], ("vy", dy, dc))
-    for dz in range(1, NZ):
-        send(lambda: table.at[z], lambda dz=dz: at(dz=dz), ("vz", dz))
-    for dz in range(1, NZ):
-        arrive(table.at[mod(z - dz, NZ)], ("vz", dz))
-    table_ref[...] = table[...]
+    table[chip, core] = (parts[0] + parts[1]) + (parts[2] + parts[3])
+    steps = [(dy, dz) for dz in range(NZ) for dy in range(NY) if (dy, dz) != (0, 0)]
+    for dy, dz in steps:
+        send(lambda: table.at[chip, core], lambda dy=dy, dz=dz: at(dy=dy, dz=dz), ("vp", dy, dz))
+    for dy, dz in steps:
+        arrive(table.at[mod(y - dy, NY) * NZ + mod(z - dz, NZ), core], ("vp", dy, dz))
+    send(lambda: table.at[:, core], lambda: at(dc=1), ("vc",))
+    arrive(table.at[:, lax.rem(core + 1, 2)], ("vc",))
+
+    order = order_ref[...]
+    rows = table[...].reshape(NROWS, HALF)
+    lane = lax.broadcasted_iota(jnp.int32, (HALF, B), 0)
+    pick = jnp.where(lane == order % HALF, 1.0, 0.0).astype(jnp.bfloat16)
+    picked = jnp.zeros((NROWS, B), jnp.float32)
+    for _ in range(3):
+        piece = rows.astype(jnp.bfloat16)
+        rows = rows - piece.astype(jnp.float32)
+        picked = picked + jnp.dot(piece, pick, preferred_element_type=jnp.float32)
+    line = lax.broadcasted_iota(jnp.int32, (NROWS, B), 0)
+    variance_ref[...] = jnp.sum(jnp.where(line == order // HALF, picked, 0.0), axis=0, keepdims=True)
     for op in pending:
         op().wait_send()
     assert len(sends) <= SEMS and len(recvs) <= SEMS
 
 
 SEMS = 240
-
-
-def tile_slots(subtree):
-    upper, middle, lower = subtree // 8, subtree // 4, subtree // 2
-    i4 = jnp.arange(4, dtype=jnp.int32)
-    i2 = jnp.arange(2, dtype=jnp.int32)
-    i8 = jnp.arange(8, dtype=jnp.int32)
-    rows = jnp.concatenate([i8, 8 + 4 * upper + i4, 16 + 2 * middle + i2, 24 + lower[None]])
-    z = rows % 8
-    base = FAR_BASE + z * COLUMN
-    near_part = rows[:, None] * NEAR + jnp.arange(NEAR, dtype=jnp.int32)
-    first = jnp.where(upper == 0, near_part[:8], jnp.concatenate(
-        [near_part[:8, :8], base[:8, None] + i4], axis=1))
-    near_part = jnp.concatenate([first, near_part[8:]], axis=0)
-    far0 = base[:8, None] + jnp.concatenate([4 + 2 * middle + i2, 12 + lower[None]])
-    far1 = base[8:12, None] + jnp.concatenate(
-        [20 + 2 * (middle - 2 * upper) + i2, 24 + (lower - 4 * upper)[None]])
-    far2 = base[12:14, None] + jnp.concatenate([28 + i2, 30 + (lower - 2 * middle)[None]])
-    far3 = base[14:, None] + jnp.arange(32, 35, dtype=jnp.int32)
-    far_part = jnp.concatenate([far0, far1, far2, far3], axis=0)
-    return jnp.concatenate([near_part, far_part], axis=1).reshape(-1).astype(jnp.int32)
+HALF = B // 2
+NROWS = NY * NZ * 2 * 2 * DESC
 
 
 def body(sigma_tiles, panel_factor, panel_mask, inv_diagonal, subtree_of, partition_order):
-    leaf = lax.axis_index("leaf")
-    x = lax.axis_index("panel")
-    slots = tile_slots(subtree_of[leaf])
-    mine = (jnp.arange(B) // Q == x)[None, :]
-    inverse = jnp.where(mine, jnp.tile(inv_diagonal, (1, NX)), 0.0)
-    covariance, table = pl.pallas_call(
+    product, variance = pl.pallas_call(
         kernel,
         out_shape=(
             jax.ShapeDtypeStruct((DESC, CH, Q, B), jnp.bfloat16),
-            jax.ShapeDtypeStruct((NZ, NY, 2, DESC, B), jnp.float32),
+            jax.ShapeDtypeStruct((1, B), jnp.float32),
         ),
         in_specs=[
             pl.BlockSpec(memory_space=pltpu.SMEM),
             pl.BlockSpec(memory_space=pltpu.SMEM),
+            pl.BlockSpec(memory_space=pltpu.VMEM),
             pl.BlockSpec(memory_space=pltpu.VMEM),
             pl.BlockSpec(memory_space=pl.ANY),
             pl.BlockSpec(memory_space=pl.ANY),
@@ -425,8 +442,8 @@
             pltpu.VMEM((CH * Q, CH * B), jnp.bfloat16),
             pltpu.VMEM((DESC, CH, B, B), jnp.bfloat16),
             pltpu.VMEM((DESC, CH, Q, B), jnp.bfloat16),
-            pltpu.VMEM((NX, DESC, B), jnp.float32),
-            pltpu.VMEM((NZ, NY, 2, DESC, B), jnp.float32),
+            pltpu.VMEM((NX, 2 * DESC, HALF), jnp.float32),
+            pltpu.VMEM((NY * NZ, 2, 2 * DESC, HALF), jnp.float32),
             pltpu.SemaphoreType.DMA((SEMS,)),
             pltpu.SemaphoreType.DMA((SEMS,)),
             pltpu.SemaphoreType.DMA((2 * DESC + 2,)),
@@ -434,13 +451,8 @@
         compiler_params=pltpu.CompilerParams(
             collective_id=0, has_side_effects=True, vmem_limit_bytes=58 * 1024 * 1024
         ),
-    )(slots, panel_mask, inverse, sigma_tiles, panel_factor)
-    column = partition_order % B
-    block = partition_order // B
-    owner, j = block // DESC, block % DESC
-    place = (((owner // 2 % NZ * NY + owner // 2 // NZ) * 2 + owner % 2) * DESC + j) * B + column
-    variance = jnp.take(table.reshape(-1), place, axis=0)
-    return covariance, variance
+    )(subtree_of, panel_mask, inv_diagonal, partition_order.reshape(1, B), sigma_tiles, panel_factor)
+    return -product, variance.reshape(B)
 
 
 def solution(mesh):

time: 131 us -> 115 us (0.88)
  local copies, waits for them, and re-layouts: 9.36 us -> 0.57 us
  Pallas kernels: 115 us -> 111 us
  between operations: 3.37 us -> 0.65 us
    pallas_call x1, Pallas kernels: 115 us -> 111 us  [body(): pl.pallas_call(kernel, out_shape=(jax.ShapeDtypeStruct((DESC, CH, Q, B),...]
    unnamed x4 -> x3, local copies, waits for them, and re-layouts: 4.13 us -> 0.57 us
    neg x0 -> x1, other arithmetic: none -> 3.35 us  [body(): return (-product, variance.reshape(B))]
    gather x1 -> x0, local copies, waits for them, and re-layouts: 1.72 us -> none  [body(): variance = jnp.take(table.reshape(-1), place, axis=0)]
    select_n x4 -> x0, other arithmetic: 1.33 us -> none  [the longest x2 0.65 us: body(): variance = jnp.take(table.reshape(-1), place, axis=0)]
where the time goes in v2:
time: 115 us
  Pallas kernels  111 us (97%)
  other arithmetic  3.35 us (3%)
    pallas_call x1, Pallas kernels, body(): pl.pallas_call(kernel, out_shape=(jax.ShapeDtypeStruct((DESC, CH, Q, B),...  111 us
    neg x1, other arithmetic, body(): return (-product, variance.reshape(B))  3.35 us

profile of v2, /device:TPU:1, one launch (start us, length us, event | category | flops | bytes accessed | tf_op | source)
XLA Modules:
  0.0 115.3 jit_solution(15162174096767379557)
XLA Ops:
  0.6 110.7 %shard_map.77 = (bf16[4,15,64,256]{3,2,1,0:T(8,128)(2,1)}, f32[1,256]{1,0:T(1,128)}) custom-call(s32[64]{0:T(128)} %subtree_ref.1, s32[4,15]{1,0:T(4,128)} %mask_ref.1, f32[4,64]{1,0:T(4,128)} %inv_ref.1, s32[1,256]{1,0:T(1,128)} %bitcast.2, bf16[16,64,256]{2,1,0:T(8,128)(2,1)} %sigma_ref.1, bf16[4,15,64,256]{3,2,1,0:T(8,128)(2,1)} %factor_ref.1), custom_call_target="tpu_custom_call" | custom-call | tf_op jit(solution)/shard_map/pallas_call | solution.py:422
  111.3 0.0 copy-start
  111.3 3.4 %neg.3 = bf16[4,15,64,256]{3,2,1,0:T(8,128)(2,1)} negate(bf16[4,15,64,256]{3,2,1,0:T(8,128)(2,1)} %get-tuple-element.4) | non-fusion elementwise | flops 983040 | bytes 3932160 | tf_op jit(solution)/shard_map/neg | solution.py:455
  114.7 0.0 copy-done
  114.7 0.6 copy.9
Async XLA Ops:
  111.3 3.4 %copy-start = (f32[1,256]{1,0:T(1,128)S(1)}, f32[1,256]{1,0:T(1,128)}, u32[]{:S(2)}) copy-start(f32[1,256]{1,0:T(1,128)} %get-tuple-element.5) | copy-start | bytes 3076

commit v3 on v2

--- a/solution.py
+++ b/solution.py
@@ -73,13 +73,52 @@
     def arrive(ref, name):
         copy(ref, ref, beside(1), name).wait_recv()
 
-    for j in range(DESC):
-        pltpu.make_async_copy(factor_ref.at[j], own.at[j], local_sem.at[j]).start()
-
     peers = [beside(1), beside(-1), at(dy=1), at(dy=-1), at(dz=1), at(dz=-1), at(dc=1)]
     barrier = pltpu.get_barrier_semaphore()
     for peer in peers:
         pl.semaphore_signal(barrier, inc=1, device_id=peer, device_id_type=MESH)
+
+    def near(dy, dz, low=0, count=NEAR):
+        row = mod(y + dy, NY) * NZ + mod(z + dz, NZ)
+        return tiles.at[pl.ds(row * NEAR + low, count)]
+
+    def far(dz, low=0, count=COLUMN):
+        return tiles.at[pl.ds(FAR_BASE + mod(z + dz, NZ) * COLUMN + low, count)]
+
+    def own_tiles(pieces):
+        ops = [
+            pltpu.make_async_copy(sigma_ref.at[pl.ds(src, ref.shape[0])], ref, local_sem.at[2 * DESC + k])
+            for k, (src, ref) in enumerate(pieces)
+        ]
+        for op in ops:
+            op.start()
+        for op in ops:
+            op.wait()
+
+    for j in range(DESC):
+        pltpu.make_async_copy(factor_ref.at[j], own.at[j], local_sem.at[j]).start()
+
+    @pl.when(core == 0)
+    def _():
+        group = jnp.where(y == 0, 0, z // 4)
+        own_tiles([(0, near(0, 0, 0, 8)), (8 + 4 * group, near(0, 0, 8, 4))])
+
+    for c in range(NY):
+        @pl.when((core == 1) & (y == c))
+        def _():
+            if c == 0:
+                own_tiles([(0, far(0, 4, 16))])
+            elif c == 1:
+                own_tiles([(4 * (z // 4), far(0, 20, 4)), (8 + 4 * (z // 4), far(0, 24, 4))])
+            elif c == 2:
+                own_tiles([(2 * (z // 2), far(0, 28, 2)), (8 + 2 * (z // 2), far(0, 30, 2))])
+            else:
+                own_tiles([(2 * (z // 2), far(0, 32, 2)), (8 + z, far(0, 34, 1))])
+
+    for j in range(DESC):
+        pltpu.make_async_copy(factor_ref.at[j], own.at[j], local_sem.at[j]).wait()
+        for b in range(CH):
+            own[j, b] = own[j, b] * mask_ref[j, b].astype(jnp.bfloat16)
     pl.semaphore_wait(barrier, len(peers))
 
     def quarter(j, dx, low=0, count=CH):
@@ -90,12 +129,6 @@
         return (0, first), (first, CH - first)
 
     def factor_start(j):
-        pltpu.make_async_copy(factor_ref.at[j], own.at[j], local_sem.at[j]).wait()
-
-        @pl.loop(0, CH)
-        def _(b):
-            own[j, b] = own[j, b] * mask_ref[j, b].astype(jnp.bfloat16)
-
         send(lambda: quarter(j, 0), lambda: beside(1), ("fr", j), src=lambda: own.at[j])
         send(lambda: quarter(j, 0), lambda: beside(-1), ("fl", j), src=lambda: own.at[j])
         pltpu.make_async_copy(own.at[j], quarter(j, 0), local_sem.at[DESC + j]).start()
@@ -113,13 +146,6 @@
         arrive(quarter(j, 2, *left), ("fl2", j))
         pltpu.make_async_copy(own.at[j], quarter(j, 0), local_sem.at[DESC + j]).wait()
 
-    def near(dy, dz, low=0, count=NEAR):
-        row = mod(y + dy, NY) * NZ + mod(z + dz, NZ)
-        return tiles.at[pl.ds(row * NEAR + low, count)]
-
-    def far(dz, low=0, count=COLUMN):
-        return tiles.at[pl.ds(FAR_BASE + mod(z + dz, NZ) * COLUMN + low, count)]
-
     first6, last6 = halves(NEAR)
     near_chunks = [(dy, dz) for dy in range(NY) for dz in Z_ORDER]
 
@@ -138,15 +164,6 @@
                 ref = far(0, 0, 4)
                 copy(sigma_ref.at[pl.ds(12, 4)], ref, at(dc=1), ("extra",)).start()
 
-            upper = jnp.where(y == 0, 0, z // 4)
-            one = pltpu.make_async_copy(sigma_ref.at[pl.ds(0, 8)], near(0, 0, 0, 8), local_sem.at[2 * DESC])
-            two = pltpu.make_async_copy(
-                sigma_ref.at[pl.ds(8 + 4 * upper, 4)], near(0, 0, 8, 4), local_sem.at[2 * DESC + 1]
-            )
-            one.start()
-            two.start()
-            one.wait()
-            two.wait()
             send(lambda: near(0, 0), lambda: at(dz=1), ("zr", 1))
             send(lambda: near(0, 0), lambda: at(dz=-1), ("zl", 1))
             along_y(0)
@@ -183,136 +200,156 @@
             arrive(near(2, dz, *last6), ("yd2", dz))
             to_peer(2, dz)
 
-        events = [(0, 0, start), (0, 1, lambda: factor_start(0))]
+        events = [(0, 0, lambda: factor_start(0)), (0, 1, start)]
         events += [(0, 2 + j, lambda j=j: factor_start(j)) for j in range(1, DESC)]
         events += [(5 * d, 1, lambda d=d: ring(d)) for d in range(1, 4)]
         events += [(17, 1, ring_end)]
         for k, dz in enumerate(Z_ORDER):
             events += [(6 * (k + 1), 2, lambda dz=dz: cross(dz)), (6 * (k + 2), 3, lambda dz=dz: cross_end(dz))]
-        events += [(15 * j + 11, 4, lambda j=j: factor_forward(j)) for j in range(DESC)]
+        events += [(11 * j + 15, 4, lambda j=j: factor_forward(j)) for j in range(DESC)]
         for _, _, event in sorted(events, key=lambda e: e[:2]):
             event()
         for dz in Z_ORDER:
-            arrive(far(dz, 0, FAR[0]), ("a", dz))
-            arrive(far(dz, FAR[0], COLUMN - FAR[0]), ("b", dz))
-        for op in pending:
+            for which in range(2):
+                low, count = halves(FAR[0])[which]
+                arrive(far(dz, low, count), ("p", "0" + "ab"[which], dz))
+            for c in range(1, NY):
+                arrive(far(dz, FAR_AT[c], FAR[c]), ("p", str(c), dz))
+
+    def finish_core0():
+        for op in sent[0]:
             op().wait_send()
 
         @pl.when(y == 0)
         def _():
             copy(sigma_ref.at[pl.ds(12, 4)], far(0, 0, 4), at(dc=1), ("extra",)).wait_send()
 
+    later = []
+
     def run_core1():
-        piece = {"a": (0, FAR[0]), "b": (FAR[0], COLUMN - FAR[0])}
-
-        def sub(name, which):
-            low, count = piece[name]
-            at_low, at_count = halves(count)[which]
-            return (low + at_low, at_count)
-
-        def around(name):
-            send(lambda: far(0, *piece[name]), lambda: at(dz=1), ("zr" + name, 1))
-            send(lambda: far(0, *piece[name]), lambda: at(dz=-1), ("zl" + name, 1))
-            send(lambda: far(0, *piece[name]), lambda: at(dc=1), (name, 0))
-
-        later = []
-
-        def only(condition, action):
+        def part(c, which):
+            low, count = halves(FAR[c])[which]
+            return (FAR_AT[c] + low, count)
+
+        def only(row, action):
             before = len(pending)
 
-            @pl.when(condition)
+            @pl.when(y == row)
             def _():
                 action()
 
             for op in pending[before:]:
-                later.append((condition, op))
+                later.append((row, op))
             del pending[before:]
 
+        def around(c, which):
+            low, count = part(c, which) if c == 0 else (FAR_AT[c], FAR[c])
+            name = piece_name(c, which)
+            send(lambda: far(0, low, count), lambda: at(dz=1), ("zr" + name, 1))
+            send(lambda: far(0, low, count), lambda: at(dz=-1), ("zl" + name, 1))
+            send(lambda: far(0, low, count), lambda: at(dc=1), ("p", name, 0))
+
+        def piece_name(c, which):
+            return "0" + "ab"[which] if c == 0 else str(c)
+
+        def across_send(c, which, up):
+            send(lambda: far(0, *part(c, which)), lambda: at(dy=1 if up else -1), ("c", up, which))
+
         def load_own(c):
+            across_send(c, 1, False)
             if c == 0:
-                pieces = [(0, 4, 16)]
-            elif c == 1:
-                pieces = [(4 * (z // 4), 20, 4), (8 + 4 * (z // 4), 24, 4)]
-            elif c == 2:
-                pieces = [(2 * (z // 2), 28, 2), (8 + 2 * (z // 2), 30, 2)]
-            else:
-                pieces = [(2 * (z // 2), 32, 2), (8 + z, 34, 1)]
-            ops = [
-                pltpu.make_async_copy(
-                    sigma_ref.at[pl.ds(src, count)], far(0, dst, count), local_sem.at[2 * DESC + k]
-                )
-                for k, (src, dst, count) in enumerate(pieces)
-            ]
-            for op in ops:
-                op.start()
-            for op in ops:
-                op.wait()
+                around(0, 1)
+                arrive(far(0, 0, 4), ("extra",))
+            across_send(c, 0, True)
+            across_send(c, 0, False)
+            across_send(c, 1, True)
+            around(c, 0)
+
+        def from_below(c):
+            arrive(far(0, *part(c, 0)), ("c", True, 0))
+            send(lambda: far(0, *part(c, 0)), lambda: at(dy=1), ("c2", 0))
+
+        def from_above(c):
+            arrive(far(0, *part(c, 1)), ("c", False, 1))
+            send(lambda: far(0, *part(c, 1)), lambda: at(dy=-1), ("c2", 1))
+
+        def rest_below(c):
             if c == 0:
-                arrive(far(0, 0, 4), ("extra",))
-            send(lambda: far(0, FAR_AT[c], FAR[c]), lambda: at(dy=1), ("cu",))
-            send(lambda: far(0, FAR_AT[c], FAR[c]), lambda: at(dy=-1), ("cd",))
-
-        def from_below(c):
-            low, count = halves(FAR[c])[0]
-            arrive(far(0, FAR_AT[c], FAR[c]), ("cu",))
-            send(lambda: far(0, FAR_AT[c] + low, count), lambda: at(dy=1), ("cu2",))
-
-        def from_above(c):
-            low, count = halves(FAR[c])[1]
-            arrive(far(0, FAR_AT[c], FAR[c]), ("cd",))
-            send(lambda: far(0, FAR_AT[c] + low, count), lambda: at(dy=-1), ("cd2",))
+                around(0, 0)
+            arrive(far(0, *part(c, 1)), ("c", True, 1))
+            around(c, 1)
+
+        def rest_above(c):
+            if c == 0:
+                around(0, 1)
+            arrive(far(0, *part(c, 0)), ("c", False, 0))
+            around(c, 0)
 
         def from_two(c):
-            for (low, count), name in zip(halves(FAR[c]), (("cu2",), ("cd2",))):
-                arrive(far(0, FAR_AT[c] + low, count), name)
+            arrive(far(0, *part(c, 1)), ("c2", 1))
+            if c == 0:
+                around(0, 1)
+            arrive(far(0, *part(c, 0)), ("c2", 0))
+            around(c, 0)
 
         def start():
             for c in range(NY):
-                only(y == c, lambda c=c: load_own(c))
+                only(c, lambda c=c: load_own(c))
 
         def across():
-            for c in range(NY):
-                only(y == (c + 1) % NY, lambda c=c: from_below(c))
-            for c in range(NY):
-                only(y == (c - 1) % NY, lambda c=c: from_above(c))
-            only(y != 2, lambda: around("a"))
+            for action, dy in ((from_below, 1), (from_above, -1), (rest_below, 1), (rest_above, -1)):
+                for c in range(NY):
+                    only((c + dy) % NY, lambda c=c, action=action: action(c))
 
         def across_end():
             for c in range(NY):
-                only(y == (c + 2) % NY, lambda c=c: from_two(c))
-            only(y == 2, lambda: around("a"))
-            around("b")
+                only((c + 2) % NY, lambda c=c: from_two(c))
+
+        rings = {
+            "0a": (part(0, 0), part(0, 0), None),
+            "0b": (part(0, 1), None, part(0, 1)),
+        }
+        for c in range(1, NY):
+            rings[str(c)] = ((FAR_AT[c], FAR[c]), part(c, 0), part(c, 1))
 
         def ring(name, d):
-            arrive(far(-d, *piece[name]), ("zr" + name, d))
-            right = piece[name] if d < 3 else sub(name, 0)
-            send(lambda: far(-d, *right), lambda: at(dz=1), ("zr" + name, d + 1))
-            arrive(far(d, *piece[name]), ("zl" + name, d))
-            left = piece[name] if d < 3 else sub(name, 1)
-            send(lambda: far(d, *left), lambda: at(dz=-1), ("zl" + name, d + 1))
-            send(lambda: far(-d, *piece[name]), lambda: at(dc=1), (name, -d))
-            send(lambda: far(d, *piece[name]), lambda: at(dc=1), (name, d))
+            whole, right, left = rings[name]
+            arrive(far(-d, *whole), ("zr" + name, d))
+            right = whole if d < 3 else right
+            if right:
+                send(lambda: far(-d, *right), lambda: at(dz=1), ("zr" + name, d + 1))
+            arrive(far(d, *whole), ("zl" + name, d))
+            left = whole if d < 3 else left
+            if left:
+                send(lambda: far(d, *left), lambda: at(dz=-1), ("zl" + name, d + 1))
+            send(lambda: far(-d, *whole), lambda: at(dc=1), ("p", name, -d))
+            send(lambda: far(d, *whole), lambda: at(dc=1), ("p", name, d))
 
         def ring_end(name):
-            arrive(far(4, *sub(name, 0)), ("zr" + name, 4))
-            arrive(far(4, *sub(name, 1)), ("zl" + name, 4))
-            send(lambda: far(4, *piece[name]), lambda: at(dc=1), (name, 4))
-
-        events = [(0, 0, start), (0, 1, lambda: factor_start(0))]
+            whole, right, left = rings[name]
+            if right:
+                arrive(far(4, *right), ("zr" + name, 4))
+            if left:
+                arrive(far(4, *left), ("zl" + name, 4))
+            send(lambda: far(4, *whole), lambda: at(dc=1), ("p", name, 4))
+
+        events = [(0, 0, lambda: factor_start(0)), (0, 1, start)]
         events += [(0, 2 + j, lambda j=j: factor_start(j)) for j in range(1, DESC)]
         events += [(5, 1, across), (8, 1, across_end)]
-        for k, name in enumerate("ab"):
-            events += [(11 + 12 * d + 5 * k, 1, lambda d=d, name=name: ring(name, d)) for d in range(1, 4)]
-            events += [(54 + k, 1, lambda name=name: ring_end(name))]
-        events += [(15 * j + 11, 4, lambda j=j: factor_forward(j)) for j in range(DESC)]
+        for k, name in enumerate(RING_ORDER):
+            events += [(11 + 12 * d + 2 * k, 1, lambda d=d, name=name: ring(name, d)) for d in range(1, 4)]
+            events += [(59 + k, 1, lambda name=name: ring_end(name))]
+        events += [(11 * j + 15, 4, lambda j=j: factor_forward(j)) for j in range(DESC)]
         for _, _, event in sorted(events, key=lambda e: e[:2]):
             event()
         for dy, dz in near_chunks:
             arrive(near(dy, dz), ("n", dy, dz))
-        for op in pending:
+
+    def finish_core1():
+        for op in sent[1]:
             op().wait_send()
-        for condition, op in later:
-            @pl.when(condition)
+        for row, op in later:
+            @pl.when(y == row)
             def _():
                 op().wait_send()
 
@@ -320,12 +357,14 @@
     def _():
         run_core0()
 
+    sent = [list(pending)]
     pending.clear()
 
     @pl.when(core == 1)
     def _():
         run_core1()
 
+    sent.append(list(pending))
     pending.clear()
 
     subtree = subtree_ref[leaf]
@@ -410,10 +449,20 @@
     variance_ref[...] = jnp.sum(jnp.where(line == order // HALF, picked, 0.0), axis=0, keepdims=True)
     for op in pending:
         op().wait_send()
+
+    @pl.when(core == 0)
+    def _():
+        finish_core0()
+
+    @pl.when(core == 1)
+    def _():
+        finish_core1()
+
     assert len(sends) <= SEMS and len(recvs) <= SEMS
 
 
 SEMS = 240
+RING_ORDER = ("1", "2", "3", "0b", "0a")
 HALF = B // 2
 NROWS = NY * NZ * 2 * 2 * DESC
 
@@ -449,7 +498,7 @@
             pltpu.SemaphoreType.DMA((2 * DESC + 2,)),
         ],
         compiler_params=pltpu.CompilerParams(
-            collective_id=0, has_side_effects=True, vmem_limit_bytes=58 * 1024 * 1024
+            collective_id=0, has_side_effects=True, vmem_limit_bytes=44 * 1024 * 1024
         ),
     )(subtree_of, panel_mask, inv_diagonal, partition_order.reshape(1, B), sigma_tiles, panel_factor)
     return -product, variance.reshape(B)

time: 115 us -> 110 us (0.957)
  Pallas kernels: 111 us -> 102 us
  local copies, waits for them, and re-layouts: 0.57 us -> 5.84 us
  other arithmetic: 3.35 us -> 1.73 us
    pallas_call x1, Pallas kernels: 111 us -> 102 us  [body(): pl.pallas_call(kernel, out_shape=(jax.ShapeDtypeStruct((DESC, CH, Q, B),...]
    unnamed x3 -> x13, local copies, waits for them, and re-layouts: 0.57 us -> 5.84 us
    neg x1, other arithmetic: 3.35 us -> 1.73 us  [body(): return (-product, variance.reshape(B))]
where the time goes in v3:
time: 110 us
  Pallas kernels  102 us (93%)
  local copies, waits for them, and re-layouts  5.84 us (5%)
  other arithmetic  1.73 us (2%)
    pallas_call x1, Pallas kernels, body(): pl.pallas_call(kernel, out_shape=(jax.ShapeDtypeStruct((DESC, CH, Q, B),...  102 us
    unnamed x13, local copies, waits for them, and re-layouts  5.84 us

profile of v3, /device:TPU:1, one launch (start us, length us, event | category | flops | bytes accessed | tf_op | source)
XLA Modules:
  0.0 109.9 jit_solution(16148720403171055122)
XLA Ops:
  0.6 0.0 copy-start
  0.6 1.5 %copy-done = bf16[4,15,64,256]{3,2,1,0:T(8,128)(2,1)S(1)} copy-done((bf16[4,15,64,256]{3,2,1,0:T(8,128)(2,1)S(1)}, bf16[4,15,64,256]{3,2,1,0:T(8,128)(2,1)}, u32[]{:S(2)}) %copy-start) | copy-done | bytes 1966104
  2.2 0.0 copy-start.1
  2.2 1.0 copy-done.1
  3.2 0.0 copy-start.2
  3.2 0.7 copy-done.2
  3.9 0.0 copy-start.3
  3.9 0.7 copy-done.3
  4.6 0.0 copy-start.4
  4.6 0.7 copy-done.4
  5.3 0.0 copy-start.5
  5.3 0.7 copy-done.5
  5.9 101.7 %shard_map.77 = (bf16[4,15,64,256]{3,2,1,0:T(8,128)(2,1)S(1)}, f32[1,256]{1,0:T(1,128)S(1)}) custom-call(s32[64]{0:T(128)S(1)} %copy-done.5, s32[4,15]{1,0:T(4,128)S(1)} %copy-done.2, f32[4,64]{1,0:T(4,128)S(1)} %copy-done.3, s32[1,256]{1,0:T(1,128)S(1)} %bitcast.2, bf16[16,64,256]{2,1,0:T(8,128)(2,1)S(1)} %copy-done.1, bf16[4,15,64,256]{3,2,1,0:T(8,128)(2,1)S(1)} %copy-done), custom_call_target="tpu_custom_call" | custom-call | tf_op jit(solution)/shard_map/pallas_call | solution.py:471
  107.6 1.7 %neg.3 = bf16[4,15,64,256]{3,2,1,0:T(8,128)(2,1)} negate(bf16[4,15,64,256]{3,2,1,0:T(8,128)(2,1)S(1)} %get-tuple-element.4) | non-fusion elementwise | flops 983040 | bytes 3932160 | tf_op jit(solution)/shard_map/neg | solution.py:504
  109.4 0.6 copy.9
Async XLA Ops:
  0.6 1.5 %copy-start = (bf16[4,15,64,256]{3,2,1,0:T(8,128)(2,1)S(1)}, bf16[4,15,64,256]{3,2,1,0:T(8,128)(2,1)}, u32[]{:S(2)}) copy-start(bf16[4,15,64,256]{3,2,1,0:T(8,128)(2,1)} %factor_ref.1) | copy-start | bytes 5898244
  2.2 1.0 copy-start.1
  3.2 0.7 copy-start.2
  3.9 0.7 copy-start.3
  4.6 0.7 copy-start.4
  5.3 0.7 copy-start.5

commit v4 on v3

--- a/solution.py
+++ b/solution.py
@@ -25,10 +25,11 @@
 
 
 def kernel(
-    subtree_ref, mask_ref, inv_ref, order_ref, sigma_ref, factor_ref,
+    subtree_hbm, mask_hbm, inv_hbm, order_hbm, sigma_ref, factor_ref,
     product_ref, variance_ref,
-    tiles, lhs, full, own, parts, table,
-    send_sem, recv_sem, local_sem,
+    tiles, lhs, full, own, rounded, parts, table,
+    subtree_ref, mask_ref, inv_ref, order_ref,
+    send_sem, recv_sem, local_sem, small_sem,
 ):
     leaf = lax.axis_index("leaf")
     x = lax.axis_index("panel")
@@ -97,6 +98,15 @@
 
     for j in range(DESC):
         pltpu.make_async_copy(factor_ref.at[j], own.at[j], local_sem.at[j]).start()
+
+    small = [
+        pltpu.make_async_copy(src, dst, small_sem.at[k])
+        for k, (src, dst) in enumerate((
+            (mask_hbm, mask_ref), (subtree_hbm, subtree_ref), (inv_hbm, inv_ref), (order_hbm, order_ref),
+        ))
+    ]
+    for op in small:
+        op.start()
 
     @pl.when(core == 0)
     def _():
@@ -115,6 +125,8 @@
             else:
                 own_tiles([(2 * (z // 2), far(0, 32, 2)), (8 + z, far(0, 34, 1))])
 
+    for op in small:
+        op.wait()
     for j in range(DESC):
         pltpu.make_async_copy(factor_ref.at[j], own.at[j], local_sem.at[j]).wait()
         for b in range(CH):
@@ -415,7 +427,8 @@
 
         product = jnp.dot(lhs[...], full[j].reshape(CH * B, B), preferred_element_type=jnp.float32)
         product = product.reshape(CH, Q, B)
-        product_ref[j] = product.astype(jnp.bfloat16)
+        rounded[j] = product.astype(jnp.bfloat16)
+        pltpu.make_async_copy(rounded.at[j], product_ref.at[j], local_sem.at[j]).start()
         total = jnp.sum(own[j].astype(jnp.float32) * product, axis=(0, 1), keepdims=True)[0]
         inverse = inv_ref[pl.ds(j, 1)]
         inverse = jnp.concatenate([inverse, inverse], axis=1)
@@ -447,6 +460,8 @@
         picked = picked + jnp.dot(piece, pick, preferred_element_type=jnp.float32)
     line = lax.broadcasted_iota(jnp.int32, (NROWS, B), 0)
     variance_ref[...] = jnp.sum(jnp.where(line == order // HALF, picked, 0.0), axis=0, keepdims=True)
+    for j in range(DESC):
+        pltpu.make_async_copy(rounded.at[j], product_ref.at[j], local_sem.at[j]).wait()
     for op in pending:
         op().wait_send()
 
@@ -474,16 +489,9 @@
             jax.ShapeDtypeStruct((DESC, CH, Q, B), jnp.bfloat16),
             jax.ShapeDtypeStruct((1, B), jnp.float32),
         ),
-        in_specs=[
-            pl.BlockSpec(memory_space=pltpu.SMEM),
-            pl.BlockSpec(memory_space=pltpu.SMEM),
-            pl.BlockSpec(memory_space=pltpu.VMEM),
-            pl.BlockSpec(memory_space=pltpu.VMEM),
-            pl.BlockSpec(memory_space=pl.ANY),
-            pl.BlockSpec(memory_space=pl.ANY),
-        ],
+        in_specs=[pl.BlockSpec(memory_space=pltpu.HBM)] * 6,
         out_specs=(
-            pl.BlockSpec(memory_space=pltpu.VMEM),
+            pl.BlockSpec(memory_space=pltpu.HBM),
             pl.BlockSpec(memory_space=pltpu.VMEM),
         ),
         scratch_shapes=[
@@ -491,14 +499,20 @@
             pltpu.VMEM((CH * Q, CH * B), jnp.bfloat16),
             pltpu.VMEM((DESC, CH, B, B), jnp.bfloat16),
             pltpu.VMEM((DESC, CH, Q, B), jnp.bfloat16),
+            pltpu.VMEM((DESC, CH, Q, B), jnp.bfloat16),
             pltpu.VMEM((NX, 2 * DESC, HALF), jnp.float32),
             pltpu.VMEM((NY * NZ, 2, 2 * DESC, HALF), jnp.float32),
+            pltpu.SMEM((NY * NZ * 2,), jnp.int32),
+            pltpu.SMEM((DESC, CH), jnp.int32),
+            pltpu.VMEM((DESC, Q), jnp.float32),
+            pltpu.VMEM((1, B), jnp.int32),
             pltpu.SemaphoreType.DMA((SEMS,)),
             pltpu.SemaphoreType.DMA((SEMS,)),
             pltpu.SemaphoreType.DMA((2 * DESC + 2,)),
+            pltpu.SemaphoreType.DMA((4,)),
         ],
         compiler_params=pltpu.CompilerParams(
-            collective_id=0, has_side_effects=True, vmem_limit_bytes=44 * 1024 * 1024
+            collective_id=0, has_side_effects=True, vmem_limit_bytes=56 * 1024 * 1024
         ),
     )(subtree_of, panel_mask, inv_diagonal, partition_order.reshape(1, B), sigma_tiles, panel_factor)
     return -product, variance.reshape(B)

time: 110 us -> 107 us (0.973)
  local copies, waits for them, and re-layouts: 5.84 us -> 0.57 us
  other arithmetic: 1.73 us -> 3.35 us
    unnamed x13 -> x3, local copies, waits for them, and re-layouts: 5.84 us -> 0.57 us
    neg x1, other arithmetic: 1.73 us -> 3.35 us  [body(): return (-product, variance.reshape(B))]
where the time goes in v4:
time: 107 us; the launch traced here: 106 us
  Pallas kernels  102 us (95%)
  other arithmetic  3.35 us (3%)
    pallas_call x1, Pallas kernels, body(): pl.pallas_call(kernel, out_shape=(jax.ShapeDtypeStruct((DESC, CH, Q, B),...  102 us
    neg x1, other arithmetic, body(): return (-product, variance.reshape(B))  3.35 us

profile of v4, /device:TPU:1, one launch (start us, length us, event | category | flops | bytes accessed | tf_op | source)
XLA Modules:
  0.0 106.4 jit_solution(2834935511954185911)
XLA Ops:
  0.6 101.9 %shard_map.77 = (bf16[4,15,64,256]{3,2,1,0:T(8,128)(2,1)}, f32[1,256]{1,0:T(1,128)}) custom-call(s32[64]{0:T(128)} %subtree_hbm.1, s32[4,15]{1,0:T(4,128)} %mask_hbm.1, f32[4,64]{1,0:T(4,128)} %inv_hbm.1, s32[1,256]{1,0:T(1,128)} %bitcast.2, bf16[16,64,256]{2,1,0:T(8,128)(2,1)} %sigma_ref.1, bf16[4,15,64,256]{3,2,1,0:T(8,128)(2,1)} %factor_ref.1), custom_call_target="tpu_custom_call" | custom-call | tf_op jit(solution)/shard_map/pallas_call | solution.py:486
  102.5 0.0 copy-start
  102.5 3.4 %neg.3 = bf16[4,15,64,256]{3,2,1,0:T(8,128)(2,1)} negate(bf16[4,15,64,256]{3,2,1,0:T(8,128)(2,1)} %get-tuple-element.4) | non-fusion elementwise | flops 983040 | bytes 3932160 | tf_op jit(solution)/shard_map/neg | solution.py:518
  105.9 0.0 copy-done
  105.9 0.6 copy.9
Async XLA Ops:
  102.5 3.4 %copy-start = (f32[1,256]{1,0:T(1,128)S(1)}, f32[1,256]{1,0:T(1,128)}, u32[]{:S(2)}) copy-start(f32[1,256]{1,0:T(1,128)} %get-tuple-element.5) | copy-start | bytes 3076

commit v5 on v4

--- a/solution.py
+++ b/solution.py
@@ -27,7 +27,7 @@
 def kernel(
     subtree_hbm, mask_hbm, inv_hbm, order_hbm, sigma_ref, factor_ref,
     product_ref, variance_ref,
-    tiles, lhs, full, own, rounded, parts, table,
+    tiles, lhs, full, own, rounded, parts, table, pick,
     subtree_ref, mask_ref, inv_ref, order_ref,
     send_sem, recv_sem, local_sem, small_sem,
 ):
@@ -218,7 +218,7 @@
         events += [(17, 1, ring_end)]
         for k, dz in enumerate(Z_ORDER):
             events += [(6 * (k + 1), 2, lambda dz=dz: cross(dz)), (6 * (k + 2), 3, lambda dz=dz: cross_end(dz))]
-        events += [(11 * j + 15, 4, lambda j=j: factor_forward(j)) for j in range(DESC)]
+        events += [(10 * j + 8, 4, lambda j=j: factor_forward(j)) for j in range(DESC)]
         for _, _, event in sorted(events, key=lambda e: e[:2]):
             event()
         for dz in Z_ORDER:
@@ -351,7 +351,7 @@
         for k, name in enumerate(RING_ORDER):
             events += [(11 + 12 * d + 2 * k, 1, lambda d=d, name=name: ring(name, d)) for d in range(1, 4)]
             events += [(59 + k, 1, lambda name=name: ring_end(name))]
-        events += [(11 * j + 15, 4, lambda j=j: factor_forward(j)) for j in range(DESC)]
+        events += [(10 * j + 8, 4, lambda j=j: factor_forward(j)) for j in range(DESC)]
         for _, _, event in sorted(events, key=lambda e: e[:2]):
             event()
         for dy, dz in near_chunks:
@@ -438,6 +438,18 @@
 
     for d in range(1, NX):
         send(lambda: parts.at[x], lambda d=d: beside(d), ("vx", d))
+    order = order_ref[...]
+    lane = lax.broadcasted_iota(jnp.int32, (HALF, B), 0)
+    pick[...] = jnp.where(lane == order % HALF, 1.0, 0.0).astype(jnp.bfloat16)
+
+    @pl.when(core == 0)
+    def _():
+        finish_core0()
+
+    @pl.when(core == 1)
+    def _():
+        finish_core1()
+
     for d in range(1, NX):
         arrive(parts.at[mod(x - d, NX)], ("vx", d))
     table[chip, core] = (parts[0] + parts[1]) + (parts[2] + parts[3])
@@ -449,15 +461,12 @@
     send(lambda: table.at[:, core], lambda: at(dc=1), ("vc",))
     arrive(table.at[:, lax.rem(core + 1, 2)], ("vc",))
 
-    order = order_ref[...]
     rows = table[...].reshape(NROWS, HALF)
-    lane = lax.broadcasted_iota(jnp.int32, (HALF, B), 0)
-    pick = jnp.where(lane == order % HALF, 1.0, 0.0).astype(jnp.bfloat16)
     picked = jnp.zeros((NROWS, B), jnp.float32)
     for _ in range(3):
         piece = rows.astype(jnp.bfloat16)
         rows = rows - piece.astype(jnp.float32)
-        picked = picked + jnp.dot(piece, pick, preferred_element_type=jnp.float32)
+        picked = picked + jnp.dot(piece, pick[...], preferred_element_type=jnp.float32)
     line = lax.broadcasted_iota(jnp.int32, (NROWS, B), 0)
     variance_ref[...] = jnp.sum(jnp.where(line == order // HALF, picked, 0.0), axis=0, keepdims=True)
     for j in range(DESC):
@@ -465,19 +474,11 @@
     for op in pending:
         op().wait_send()
 
-    @pl.when(core == 0)
-    def _():
-        finish_core0()
-
-    @pl.when(core == 1)
-    def _():
-        finish_core1()
-
     assert len(sends) <= SEMS and len(recvs) <= SEMS
 
 
 SEMS = 240
-RING_ORDER = ("1", "2", "3", "0b", "0a")
+RING_ORDER = ("0b", "0a", "1", "2", "3")
 HALF = B // 2
 NROWS = NY * NZ * 2 * 2 * DESC
 
@@ -502,6 +503,7 @@
             pltpu.VMEM((DESC, CH, Q, B), jnp.bfloat16),
             pltpu.VMEM((NX, 2 * DESC, HALF), jnp.float32),
             pltpu.VMEM((NY * NZ, 2, 2 * DESC, HALF), jnp.float32),
+            pltpu.VMEM((HALF, B), jnp.bfloat16),
             pltpu.SMEM((NY * NZ * 2,), jnp.int32),
             pltpu.SMEM((DESC, CH), jnp.int32),
             pltpu.VMEM((DESC, Q), jnp.float32),

time: 107 us -> 104 us (0.972)
  Pallas kernels: 102 us -> 99.2 us
    pallas_call x1, Pallas kernels: 102 us -> 99.2 us  [body(): pl.pallas_call(kernel, out_shape=(jax.ShapeDtypeStruct((DESC, CH, Q, B),...]
where the time goes in v5:
time: 104 us
  Pallas kernels  99.2 us (95%)
  other arithmetic  3.35 us (3%)
    pallas_call x1, Pallas kernels, body(): pl.pallas_call(kernel, out_shape=(jax.ShapeDtypeStruct((DESC, CH, Q, B),...  99.2 us
    neg x1, other arithmetic, body(): return (-product, variance.reshape(B))  3.35 us

profile of v5, /device:TPU:1, one launch (start us, length us, event | category | flops | bytes accessed | tf_op | source)
XLA Modules:
  0.0 103.8 jit_solution(4601567661020139858)
XLA Ops:
  0.6 99.2 %shard_map.77 = (bf16[4,15,64,256]{3,2,1,0:T(8,128)(2,1)}, f32[1,256]{1,0:T(1,128)}) custom-call(s32[64]{0:T(128)} %subtree_hbm.1, s32[4,15]{1,0:T(4,128)} %mask_hbm.1, f32[4,64]{1,0:T(4,128)} %inv_hbm.1, s32[1,256]{1,0:T(1,128)} %bitcast.2, bf16[16,64,256]{2,1,0:T(8,128)(2,1)} %sigma_ref.1, bf16[4,15,64,256]{3,2,1,0:T(8,128)(2,1)} %factor_ref.1), custom_call_target="tpu_custom_call" | custom-call | tf_op jit(solution)/shard_map/pallas_call | solution.py:487
  99.9 0.0 copy-start
  99.9 3.4 %neg.3 = bf16[4,15,64,256]{3,2,1,0:T(8,128)(2,1)} negate(bf16[4,15,64,256]{3,2,1,0:T(8,128)(2,1)} %get-tuple-element.4) | non-fusion elementwise | flops 983040 | bytes 3932160 | tf_op jit(solution)/shard_map/neg | solution.py:520
  103.2 0.0 copy-done
  103.2 0.6 copy.9
Async XLA Ops:
  99.9 3.4 %copy-start = (f32[1,256]{1,0:T(1,128)S(1)}, f32[1,256]{1,0:T(1,128)}, u32[]{:S(2)}) copy-start(f32[1,256]{1,0:T(1,128)} %get-tuple-element.5) | copy-start | bytes 3076

commit v6 on v5

--- a/solution.py
+++ b/solution.py
@@ -217,7 +217,7 @@
         events += [(5 * d, 1, lambda d=d: ring(d)) for d in range(1, 4)]
         events += [(17, 1, ring_end)]
         for k, dz in enumerate(Z_ORDER):
-            events += [(6 * (k + 1), 2, lambda dz=dz: cross(dz)), (6 * (k + 2), 3, lambda dz=dz: cross_end(dz))]
+            events += [(5 * (k + 1) + 8, 2, lambda dz=dz: cross(dz)), (5 * (k + 1) + 20, 3, lambda dz=dz: cross_end(dz))]
         events += [(10 * j + 8, 4, lambda j=j: factor_forward(j)) for j in range(DESC)]
         for _, _, event in sorted(events, key=lambda e: e[:2]):
             event()
@@ -456,10 +456,17 @@
     steps = [(dy, dz) for dz in range(NZ) for dy in range(NY) if (dy, dz) != (0, 0)]
     for dy, dz in steps:
         send(lambda: table.at[chip, core], lambda dy=dy, dz=dz: at(dy=dy, dz=dz), ("vp", dy, dz))
-    for dy, dz in steps:
-        arrive(table.at[mod(y - dy, NY) * NZ + mod(z - dz, NZ), core], ("vp", dy, dz))
-    send(lambda: table.at[:, core], lambda: at(dc=1), ("vc",))
-    arrive(table.at[:, lax.rem(core + 1, 2)], ("vc",))
+
+    def block(dy, dz, side):
+        return table.at[mod(y - dy, NY) * NZ + mod(z - dz, NZ), lax.rem(core + side, 2)]
+
+    steps.sort(key=lambda step: min(step[0], NY - step[0]) + min(step[1], NZ - step[1]))
+    for dy, dz in [(0, 0)] + steps:
+        if (dy, dz) != (0, 0):
+            arrive(block(dy, dz, 0), ("vp", dy, dz))
+        send(lambda dy=dy, dz=dz: block(dy, dz, 0), lambda: at(dc=1), ("vc", dy, dz))
+    for dy, dz in [(0, 0)] + steps:
+        arrive(block(dy, dz, 1), ("vc", dy, dz))
 
     rows = table[...].reshape(NROWS, HALF)
     picked = jnp.zeros((NROWS, B), jnp.float32)

time: 104 us -> 104 us (level)
  no operation moved by 1% of the time
where the time goes in v6:
time: 104 us
  Pallas kernels  99.1 us (95%)
  other arithmetic  3.35 us (3%)
    pallas_call x1, Pallas kernels, body(): pl.pallas_call(kernel, out_shape=(jax.ShapeDtypeStruct((DESC, CH, Q, B),...  99.1 us
    neg x1, other arithmetic, body(): return (-product, variance.reshape(B))  3.35 us

profile of v6, /device:TPU:1, one launch (start us, length us, event | category | flops | bytes accessed | tf_op | source)
XLA Modules:
  0.0 103.7 jit_solution(1798550853877600812)
XLA Ops:
  0.6 99.1 %shard_map.77 = (bf16[4,15,64,256]{3,2,1,0:T(8,128)(2,1)}, f32[1,256]{1,0:T(1,128)}) custom-call(s32[64]{0:T(128)} %subtree_hbm.1, s32[4,15]{1,0:T(4,128)} %mask_hbm.1, f32[4,64]{1,0:T(4,128)} %inv_hbm.1, s32[1,256]{1,0:T(1,128)} %bitcast.2, bf16[16,64,256]{2,1,0:T(8,128)(2,1)} %sigma_ref.1, bf16[4,15,64,256]{3,2,1,0:T(8,128)(2,1)} %factor_ref.1), custom_call_target="tpu_custom_call" | custom-call | tf_op jit(solution)/shard_map/pallas_call | solution.py:494
  99.7 0.0 copy-start
  99.7 3.4 %neg.3 = bf16[4,15,64,256]{3,2,1,0:T(8,128)(2,1)} negate(bf16[4,15,64,256]{3,2,1,0:T(8,128)(2,1)} %get-tuple-element.4) | non-fusion elementwise | flops 983040 | bytes 3932160 | tf_op jit(solution)/shard_map/neg | solution.py:527
  103.1 0.0 copy-done
  103.1 0.6 copy.9
Async XLA Ops:
  99.7 3.4 %copy-start = (f32[1,256]{1,0:T(1,128)S(1)}, f32[1,256]{1,0:T(1,128)}, u32[]{:S(2)}) copy-start(f32[1,256]{1,0:T(1,128)} %get-tuple-element.5) | copy-start | bytes 3076
